TPU v7x, 32 devices: a whole 2x2x4 slice. The times are simulated.
32 devices in a mesh: seq: 4 (over z), head: 4 (over y, x), rep: 2 (over core).
Axes of the slice: x: 2, y: 2, z: 4, core: 2. Of those that a mesh axis runs over, the one named last changes fastest.
Arguments:
- queries: bfloat16 [64, 64, 128], P(('seq', 'head', 'rep'))
- prefix_keys: bfloat16 [16384, 4, 128], P(('seq', 'rep'), 'head')
- prefix_values: bfloat16 [16384, 4, 128], P(('seq', 'rep'), 'head'), may hold values from -6 to 6
- suffix_keys: bfloat16 [64, 2048, 4, 128], P(('seq', 'head', 'rep')), may hold values from -8.375 to 8.375
- suffix_values: bfloat16 [64, 2048, 4, 128], P(('seq', 'head', 'rep')), may hold values from -6 to 6
- suffix_lengths: int32 [64], P(('seq', 'head', 'rep')), may hold values from 256 to 2048, as said below
- slot_map: int32 [64], P(('seq', 'head', 'rep')), may hold values from 0 to 63, as said below
Outputs:
- attention: float32 [64, 64, 128], P(('seq', 'head', 'rep'))
- log_total: float32 [64, 64], P(('seq', 'head', 'rep'))
Inputs may be any that keep to these rules, and one draw needn't show every extreme that they name: `suffix_lengths`: every request has at least 256 live suffix positions, and some request has exactly 2048. slot_map is a permutation of the slots that keeps each aligned block of 2 requests in the block of 2 slots with the same indices.
All inputs are finite; a program needn't handle non-finite values.
Results may differ from a plain program's by a relative error of at most 0.00099.
Values may be sent and summed in bfloat16 or wider, within the bound.
No kernel may reach another device: no remote copies, remote signals or barrier semaphores. Data moves between devices by JAX's collectives and lax.ppermute only.
A program may use at most 64 MiB of HBM per device.

v0:
```python
import jax
import jax.numpy as jnp
from jax import lax
from jax.sharding import PartitionSpec as P


def softmax_rows(query_rows, local_keys, local_values, score_scale):
    scores = (
        jnp.einsum("qd,kd->qk", query_rows, local_keys, preferred_element_type=jnp.float32)
        * score_scale
    )
    row_max = jnp.max(scores, axis=1, keepdims=True)
    exp_terms = jnp.exp(scores - row_max)
    row_total = jnp.sum(exp_terms, axis=1, keepdims=True)
    weights = exp_terms.astype(jnp.bfloat16)
    mixed = jnp.dot(weights, local_values, preferred_element_type=jnp.float32) / row_total
    return (mixed, (row_max + jnp.log(row_total))[:, 0])


def prefix_partials(grouped_q, local_keys, local_values, score_scale):
    req_total, group_size, head_width = grouped_q.shape
    per_block = max(1, 512 // group_size)

    def one_block(block_q):
        block_rows = block_q.shape[0]
        mixed, logs = softmax_rows(
            block_q.reshape(-1, head_width), local_keys, local_values, score_scale
        )
        return (
            mixed.reshape(block_rows, group_size, head_width),
            logs.reshape(block_rows, group_size),
        )

    blocked = grouped_q.reshape(req_total // per_block, per_block, group_size, head_width)
    mixed, logs = lax.map(one_block, blocked)
    return (mixed.reshape(req_total, group_size, head_width), logs.reshape(req_total, group_size))


def join_partials(left_part, right_part):
    left_mixed, left_log = left_part
    right_mixed, right_log = right_part
    new_max = jnp.maximum(left_log, right_log)
    left_weight = jnp.exp(left_log - new_max)
    right_weight = jnp.exp(right_log - new_max)
    weight_sum = left_weight + right_weight
    mixed = (
        left_mixed * left_weight[..., None] + right_mixed * right_weight[..., None]
    ) / weight_sum[..., None]
    return (mixed, new_max + jnp.log(weight_sum))


def suffix_partials(slot_q, slot_lengths, suffix_keys, suffix_values, score_scale):
    suf_len = suffix_keys.shape[1]
    scores = (
        jnp.einsum("rghd,rsgd->rghs", slot_q, suffix_keys, preferred_element_type=jnp.float32)
        * score_scale
    )
    positions = jnp.arange(suf_len, dtype=jnp.int32)
    live_mask = positions[None, None, None, :] < slot_lengths[:, None, None, None]
    scores = jnp.where(live_mask, scores, -1e30)
    row_max = jnp.max(scores, axis=-1)
    exp_terms = jnp.where(live_mask, jnp.exp(scores - row_max[..., None]), 0.0)
    row_total = jnp.sum(exp_terms, axis=-1)
    acc = jnp.einsum(
        "rghs,rsgd->rghd",
        exp_terms.astype(jnp.bfloat16),
        suffix_values,
        preferred_element_type=jnp.float32,
    )
    return (acc / row_total[..., None], row_max + jnp.log(row_total))


def per_device(
    queries, prefix_keys, prefix_values, suffix_keys, suffix_values, suffix_lengths, slot_map
):
    req_count, head_count, head_width = queries.shape
    kv_count = suffix_keys.shape[2]
    group_size = head_count // kv_count
    score_scale = head_width ** (-0.5)
    head_devices = lax.axis_size("head")
    slot_local = slot_map % req_count
    inverse = jnp.argsort(slot_local)
    slot_q = queries[inverse].reshape(req_count, kv_count, group_size, head_width)
    slot_lengths = suffix_lengths[inverse]
    suf_mixed, suf_log = suffix_partials(
        slot_q, slot_lengths, suffix_keys, suffix_values, score_scale
    )
    suf_mixed = suf_mixed.reshape(req_count, head_count, head_width)[slot_local]
    suf_log = suf_log.reshape(req_count, head_count)[slot_local]
    local_keys = prefix_keys[:, 0, :]
    local_values = prefix_values[:, 0, :]
    head_place = lax.axis_index("head")
    own = lax.dynamic_slice_in_dim(
        lax.all_gather(queries, ("seq", "head", "rep"), axis=0, tiled=True),
        head_place * group_size,
        group_size,
        1,
    )
    pre_mixed, pre_log = prefix_partials(own, local_keys, local_values, score_scale)
    seq_devices = lax.axis_size("seq")
    rep_devices = lax.axis_size("rep")
    pre_mixed = pre_mixed.reshape(
        seq_devices, head_devices, rep_devices, req_count, group_size, head_width
    )
    pre_mixed = pre_mixed.transpose(0, 2, 1, 3, 4, 5).reshape(-1, group_size, head_width)
    pre_log = pre_log.reshape(seq_devices, head_devices, rep_devices, req_count, group_size)
    pre_log = pre_log.transpose(0, 2, 1, 3, 4).reshape(-1, group_size)
    local_rows = head_devices * req_count
    got_mixed, got_log = (
        lax.all_to_all(pre_mixed, ("seq", "rep"), split_axis=0, concat_axis=0, tiled=True),
        lax.all_to_all(pre_log, ("seq", "rep"), split_axis=0, concat_axis=0, tiled=True),
    )
    got_mixed = got_mixed.reshape(-1, local_rows, group_size, head_width)
    got_log = got_log.reshape(-1, local_rows, group_size)
    block_max = jnp.max(got_log, axis=0)
    block_weight = jnp.exp(got_log - block_max[None])
    weight_sum = jnp.sum(block_weight, axis=0)
    own_mixed = jnp.sum(block_weight[..., None] * got_mixed, axis=0) / weight_sum[..., None]
    own_log = block_max + jnp.log(weight_sum)
    back_mixed, back_log = (
        lax.all_to_all(own_mixed, "head", split_axis=0, concat_axis=1, tiled=True),
        lax.all_to_all(own_log, "head", split_axis=0, concat_axis=1, tiled=True),
    )
    attention, log_total = join_partials((suf_mixed, suf_log), (back_mixed, back_log))
    return (attention, log_total)


def solution(mesh):
    placed = (
        P(("seq", "head", "rep"), None, None),
        P(("seq", "rep"), "head", None),
        P(("seq", "rep"), "head", None),
        P(("seq", "head", "rep"), None, None, None),
        P(("seq", "head", "rep"), None, None, None),
        P(("seq", "head", "rep")),
        P(("seq", "head", "rep")),
    )
    return jax.shard_map(
        per_device,
        mesh=mesh,
        in_specs=placed,
        out_specs=(P(("seq", "head", "rep"), None, None), P(("seq", "head", "rep"), None)),
        check_vma=False,
    )
```

profile of v0, /device:TPU:0, one launch (start us, length us, event | category | flops | bytes accessed | tf_op | source)
XLA Modules:
  0.0 139.0 jit_solution(10663478502128448680)
XLA Ops:
  9.2 58.1 %all-gather.2.cloned.1.call-done = bf16[64,64,128]{2,1,0:T(8,128)(2,1)} async-done(((bf16[2,64,128]{2,1,0:T(8,128)(2,1)}), bf16[64,64,128]{2,1,0:T(8,128)(2,1)}) %all-gather.2.cloned.1.call-update) | async-done | bytes 1048592 | tf_op jit(solution)/shard_map/all_gather | solution.py:94
  67.3 1.0 constant_dynamic-slice_fusion.1
  68.3 15.7 %while.12 = (s32[]{:T(128)}, f32[2,32,16,128]{3,2,1,0:T(8,128)S(1)}, f32[2,32,16]{2,1,0:T(8,128)S(1)}, bf16[2,32,16,128]{3,2,1,0:T(8,128)(2,1)S(1)}, bf16[2048,1...) while((s32[]{:T(128)}, f32[2,32,16,128]{3,2,1,0:T(8,128)S(1)}, f32[2,32,16]{2,1,0:T(8,128)S(1)}, ...), condition=%wide.region_6.7_spmd, body=%wide.region_3.6_spmd.sunk | while | flops 545324544 | bytes 33738896 | solution.py:35
  68.3 1.9 %multiply_reduce_fusion.3 = (f32[512]{0:T(512)S(1)}, f32[512,2048]{1,0:T(8,128)S(1)}) fusion(bf16[512,128]{1,0:T(8,128)(2,1)S(1)} %bitcast.45, bf16[2048,128]{1,0:T(8,128)(2,1)} %get-tuple-element.122), kind=kOutput, calls=%fused_computation.5.clone.1 | convolution fusion | flops 270532096 | bytes 4851712 | tf_op jit(solution)/shard_map/while/body/eval_jaxpr/qd,kd->qk/dot_general | solution.py:9
  70.2 1.9 %copy-done.1 = f32[512,2048]{1,0:T(8,128)} copy-done((f32[512,2048]{1,0:T(8,128)}, f32[512,2048]{1,0:T(8,128)S(1)}, u32[]{:S(2)}) %copy-start.1) | copy-done | bytes 4194328 | tf_op jit(solution)/shard_map/while
  72.1 0.8 fusion.49
  73.1 3.0 %fusion.50 = f32[512,128]{1,0:T(8,128)S(1)} fusion(bf16[2048,128]{1,0:T(8,128)(2,1)S(1)} %copy-done.3, f32[512,2048]{1,0:T(8,128)} %copy-done.1, f32[512]{0:T(512)S(1)} %get-tuple-element.103, f32[512]{0:T(512)S(1)} %fusion.49), kind=kOutput, calls=%fused_computation.11.clone.1 | convolution fusion | flops 271646720 | bytes 4984832 | tf_op jit(solution)/shard_map/while/body/eval_jaxpr/dot_general | solution.py:16
  76.2 1.9 %multiply_reduce_fusion.3 = (f32[512]{0:T(512)S(1)}, f32[512,2048]{1,0:T(8,128)S(1)}) fusion(bf16[512,128]{1,0:T(8,128)(2,1)S(1)} %bitcast.45, bf16[2048,128]{1,0:T(8,128)(2,1)} %get-tuple-element.122), kind=kOutput, calls=%fused_computation.5.clone.1 | convolution fusion | flops 270532096 | bytes 4851712 | tf_op jit(solution)/shard_map/while/body/eval_jaxpr/qd,kd->qk/dot_general | solution.py:9
  78.1 1.9 %copy-done.1 = f32[512,2048]{1,0:T(8,128)} copy-done((f32[512,2048]{1,0:T(8,128)}, f32[512,2048]{1,0:T(8,128)S(1)}, u32[]{:S(2)}) %copy-start.1) | copy-done | bytes 4194328 | tf_op jit(solution)/shard_map/while
  80.0 0.8 fusion.49
  80.9 3.0 %fusion.50 = f32[512,128]{1,0:T(8,128)S(1)} fusion(bf16[2048,128]{1,0:T(8,128)(2,1)S(1)} %copy-done.3, f32[512,2048]{1,0:T(8,128)} %copy-done.1, f32[512]{0:T(512)S(1)} %get-tuple-element.103, f32[512]{0:T(512)S(1)} %fusion.49), kind=kOutput, calls=%fused_computation.11.clone.1 | convolution fusion | flops 271646720 | bytes 4984832 | tf_op jit(solution)/shard_map/while/body/eval_jaxpr/dot_general | solution.py:16
  84.7 3.6 %all-to-all-start = ((f32[8,1,128]{2,1,0:T(1,128)}), f32[8,1,128]{2,1,0:T(1,128)S(1)}, u32[]{:S(2)}, u32[]{:S(2)}) async-start(f32[8,1,128]{2,1,0:T(1,128)} %reshape.170), calls=%async_computation | async-start | bytes 8192 | tf_op jit(solution)/shard_map/all_to_all | solution.py:111
  88.9 4.8 %all-to-all-done = f32[8,1,128]{2,1,0:T(1,128)S(1)} async-done(((f32[8,1,128]{2,1,0:T(1,128)}), f32[8,1,128]{2,1,0:T(1,128)S(1)}, u32[]{:S(2)}, u32[]{:S(2)}) %all-to-all-start) | async-done | bytes 4128 | tf_op jit(solution)/shard_map/all_to_all | solution.py:111
  95.6 3.2 %all-to-all-start.1 = ((f32[4,2,16]{2,1,0:T(2,128)}), f32[4,2,16]{2,1,0:T(2,128)S(1)}, u32[]{:S(2)}, u32[]{:S(2)}) async-start(f32[4,2,16]{2,1,0:T(2,128)} %bitcast.10), calls=%async_computation.1 | async-start | bytes 8192 | tf_op jit(solution)/shard_map/all_to_all | solution.py:122
  99.6 0.8 copy.27
  100.4 3.2 %all-to-all-done.1 = f32[4,2,16]{2,1,0:T(2,128)S(1)} async-done(((f32[4,2,16]{2,1,0:T(2,128)}), f32[4,2,16]{2,1,0:T(2,128)S(1)}, u32[]{:S(2)}, u32[]{:S(2)}) %all-to-all-start.1) | async-done | bytes 544 | tf_op jit(solution)/shard_map/all_to_all | solution.py:122
  103.5 3.5 %all-to-all-start.2 = ((f32[64,16,128]{2,1,0:T(8,128)}), f32[64,16,128]{2,1,0:T(8,128)S(1)}, u32[]{:S(2)}, u32[]{:S(2)}) async-start(f32[64,16,128]{2,1,0:T(8,128)} %bitcast.14), calls=%async_computation.2 | async-start | bytes 1048576 | tf_op jit(solution)/shard_map/all_to_all | solution.py:110
  107.0 3.5 %fusion.34 = (f32[2,4,16]{2,1,0:T(4,128)S(1)}, f32[2,4,16,2048]{3,2,1,0:T(8,128)S(1)}) fusion(bf16[2,4,16,128]{3,2,1,0:T(8,128)(2,1)S(1)} %bitcast.51, bf16[2,2048,4,128]{3,2,1,0:T(4,128)(2,1)} %param.12, pred[2,2048]{1,0:T(4,128)(4,1)S(1)} %iota_compare_fusion), kind=kOutput, calls=%fused_computation.53 | convolution fusion | flops 67895168 | bytes 5280256 | tf_op jit(solution)/shard_map/rghd,rsgd->rghs/dot_general | solution.py:55
  111.5 3.1 %fusion.20 = f32[2,4,16,128]{3,2,1,0:T(8,128)S(1)} fusion(bf16[2,2048,4,128]{3,2,1,0:T(4,128)(2,1)} %param.13, f32[2,4,16,2048]{3,2,1,0:T(8,128)S(1)} %get-tuple-element.62, f32[2,4,16]{2,1,0:T(4,128)S(1)} %get-tuple-element.61, pred[2,2048]{1,0:T(4,128)(4,1)S(1)} %iota_compare_fusion, f32[2,4,16]{2,1,0:T(4,128)S(1)} %fusion.23), kind=kOutput, calls=%fused_computation.23 | convolution fusion | flops 67911680 | bytes 5313536 | tf_op jit(solution)/shard_map/rghs,rsgd->rghd/dot_general | solution.py:64
  115.3 7.0 %all-to-all-done.2 = f32[64,16,128]{2,1,0:T(8,128)S(1)} async-done(((f32[64,16,128]{2,1,0:T(8,128)}), f32[64,16,128]{2,1,0:T(8,128)S(1)}, u32[]{:S(2)}, u32[]{:S(2)}) %all-to-all-start.2) | async-done | bytes 524320 | tf_op jit(solution)/shard_map/all_to_all | solution.py:110
  122.5 0.7 broadcast_divide_fusion
  123.2 3.3 %all-to-all-start.3 = ((f32[8,16,128]{2,1,0:T(8,128)}), f32[8,16,128]{2,1,0:T(8,128)S(1)}, u32[]{:S(2)}, u32[]{:S(2)}) async-start(f32[8,16,128]{2,1,0:T(8,128)} %broadcast_divide_fusion), calls=%async_computation.3 | async-start | bytes 131072 | tf_op jit(solution)/shard_map/all_to_all | solution.py:121
  127.1 4.2 %all-to-all-done.3 = f32[8,16,128]{2,1,0:T(8,128)S(1)} async-done(((f32[8,16,128]{2,1,0:T(8,128)}), f32[8,16,128]{2,1,0:T(8,128)S(1)}, u32[]{:S(2)}, u32[]{:S(2)}) %all-to-all-start.3) | async-done | bytes 65568 | tf_op jit(solution)/shard_map/all_to_all | solution.py:121
  131.4 0.8 fusion.30
  (51 shorter events, 8.6 us)
Async XLA Ops:
  7.2 81.1 %copy-start = (s32[2]{0:T(128)S(1)}, s32[2]{0:T(128)}, u32[]{:S(2)}) copy-start(s32[2]{0:T(128)} %param.14) | copy-start | bytes 28
  7.2 60.1 %all-gather.2.cloned.1.call-start = ((), (), s32[]{:S(2)}) async-start(), calls=%async_computation.4 | async-start | bytes 1081344 | tf_op jit(solution)/shard_map/all_gather | solution.py:94
  68.3 30.7 %copy-start.2 = (bf16[2,64,128]{2,1,0:T(8,128)(2,1)S(1)}, bf16[2,64,128]{2,1,0:T(8,128)(2,1)}, u32[]{:S(2)}) copy-start(bf16[2,64,128]{2,1,0:T(8,128)(2,1)} %param.9) | copy-start | bytes 98308
  68.3 4.8 %copy-start.3 = (bf16[2048,128]{1,0:T(8,128)(2,1)S(1)}, bf16[2048,128]{1,0:T(8,128)(2,1)}, u32[]{:S(2)}) copy-start(bf16[2048,128]{1,0:T(8,128)(2,1)} %get-tuple-element.123) | copy-start | bytes 1572868 | tf_op jit(solution)/shard_map/while
  70.2 1.9 %copy-start.1 = (f32[512,2048]{1,0:T(8,128)}, f32[512,2048]{1,0:T(8,128)S(1)}, u32[]{:S(2)}) copy-start(f32[512,2048]{1,0:T(8,128)S(1)} %get-tuple-element.102) | copy-start | bytes 12582916 | tf_op jit(solution)/shard_map/while
  76.2 4.8 %copy-start.3 = (bf16[2048,128]{1,0:T(8,128)(2,1)S(1)}, bf16[2048,128]{1,0:T(8,128)(2,1)}, u32[]{:S(2)}) copy-start(bf16[2048,128]{1,0:T(8,128)(2,1)} %get-tuple-element.123) | copy-start | bytes 1572868 | tf_op jit(solution)/shard_map/while
  78.1 1.9 %copy-start.1 = (f32[512,2048]{1,0:T(8,128)}, f32[512,2048]{1,0:T(8,128)S(1)}, u32[]{:S(2)}) copy-start(f32[512,2048]{1,0:T(8,128)S(1)} %get-tuple-element.102) | copy-start | bytes 12582916 | tf_op jit(solution)/shard_map/while
  84.7 9.0 %all-to-all-start = ((f32[8,1,128]{2,1,0:T(1,128)}), f32[8,1,128]{2,1,0:T(1,128)S(1)}, u32[]{:S(2)}, u32[]{:S(2)}) async-start(f32[8,1,128]{2,1,0:T(1,128)} %reshape.170), calls=%async_computation | async-start | bytes 8192 | tf_op jit(solution)/shard_map/all_to_all | solution.py:111
  95.6 7.9 %all-to-all-start.1 = ((f32[4,2,16]{2,1,0:T(2,128)}), f32[4,2,16]{2,1,0:T(2,128)S(1)}, u32[]{:S(2)}, u32[]{:S(2)}) async-start(f32[4,2,16]{2,1,0:T(2,128)} %bitcast.10), calls=%async_computation.1 | async-start | bytes 8192 | tf_op jit(solution)/shard_map/all_to_all | solution.py:122
  103.5 18.8 %all-to-all-start.2 = ((f32[64,16,128]{2,1,0:T(8,128)}), f32[64,16,128]{2,1,0:T(8,128)S(1)}, u32[]{:S(2)}, u32[]{:S(2)}) async-start(f32[64,16,128]{2,1,0:T(8,128)} %bitcast.14), calls=%async_computation.2 | async-start | bytes 1048576 | tf_op jit(solution)/shard_map/all_to_all | solution.py:110
  123.2 8.1 %all-to-all-start.3 = ((f32[8,16,128]{2,1,0:T(8,128)}), f32[8,16,128]{2,1,0:T(8,128)S(1)}, u32[]{:S(2)}, u32[]{:S(2)}) async-start(f32[8,16,128]{2,1,0:T(8,128)} %broadcast_divide_fusion), calls=%async_computation.3 | async-start | bytes 131072 | tf_op jit(solution)/shard_map/all_to_all | solution.py:121
Sparse Core Ops, SparseCore 0:
  10.9 56.3 all-gather.1
where the time goes:
time: 140 us; the launch traced here: 139 us
  waiting for transfers between devices  78 us (56%)
  matrix products  16.4 us (12%)
  between operations  14.2 us (10%)
  starting transfers between devices  13.6 us (10%)
  local copies, waits for them, and re-layouts  9.72 us (7%)
  other arithmetic  6.91 us (5%)
    all_gather x1, waiting for transfers between devices, per_device(): lax.all_gather(queries, ('seq', 'head', 'rep'), axis=0, tiled=True)  58.1 us
    all_to_all x1, waiting for transfers between devices, per_device(): lax.all_to_all(pre_mixed, ('seq', 'rep'), split_axis=0, concat_axis=0, ti...  7.05 us
    dot_general x2, matrix products, softmax_rows(): jnp.dot(weights, local_values, preferred_element_type=jnp.float32)  6.06 us
    all_to_all x1, waiting for transfers between devices, per_device(): lax.all_to_all(pre_log, ('seq', 'rep'), split_axis=0, concat_axis=0, tile...  4.83 us
    all_to_all x1, waiting for transfers between devices, per_device(): lax.all_to_all(own_mixed, 'head', split_axis=0, concat_axis=1, tiled=True)  4.23 us
    while x8, local copies, waits for them, and re-layouts  3.87 us
    dot_general x2, matrix products, softmax_rows(): jnp.einsum('qd,kd->qk', query_rows, local_keys, preferred_element_type=jn...  3.78 us
    all_to_all x1, starting transfers between devices, per_device(): lax.all_to_all(pre_log, ('seq', 'rep'), split_axis=0, concat_axis=0, tile...  3.56 us
  transfers between devices with their start and end apart: 5, of which 5 were waited for; matrix products, arithmetic and copies ran while one was open for 9% of the time, Pallas kernels for 0%

commit v1 on v0

v1 whole, which is shorter than its diff:
```python
import functools
import math

import jax
import jax.numpy as jnp
from jax import lax
from jax.experimental import pallas as pl
from jax.experimental.pallas import tpu as pltpu
from jax.sharding import PartitionSpec as P

ROW_TILE = 128
STEP_ROWS = 512
SUF_CHUNK = 1024
LOG_ROWS = 8
NT = (((1,), (1,)), ((), ()))
VMEM_BYTES = 48 * 1024 * 1024


def suffix_kernel(
    slot_ref, length_ref, q_ref, k_ref, v_ref, mixed_ref, log_ref, score_ref, *, kv_count, score_scale
):
    heads, width = q_ref.shape[1], q_ref.shape[2]
    rows = k_ref.shape[1]
    limit = length_ref[pl.program_id(0)] * kv_count
    query = q_ref[0]
    lane = lax.broadcasted_iota(jnp.int32, (heads, SUF_CHUNK), 1)
    group = lax.broadcasted_iota(jnp.int32, (heads, SUF_CHUNK), 0) // (heads // kv_count)
    own_head = (lane % kv_count) == group
    peak = jnp.full((heads, SUF_CHUNK), -1e30, jnp.float32)
    for begin in range(0, rows, SUF_CHUNK):
        part = lax.dot_general(
            query, k_ref[0, begin : begin + SUF_CHUNK], NT, preferred_element_type=jnp.float32
        )
        part = jnp.where(own_head & (lane < limit - begin), part, -1e30)
        score_ref[:, begin : begin + SUF_CHUNK] = part
        peak = jnp.maximum(peak, part)
    row_max = jnp.max(peak, axis=1, keepdims=True)
    sums = jnp.zeros((heads, SUF_CHUNK), jnp.float32)
    acc = jnp.zeros((heads, width), jnp.float32)
    for begin in range(0, rows, SUF_CHUNK):
        terms = jnp.exp((score_ref[:, begin : begin + SUF_CHUNK] - row_max) * score_scale)
        sums = sums + terms
        acc = acc + jnp.dot(
            terms.astype(jnp.bfloat16),
            v_ref[0, begin : begin + SUF_CHUNK],
            preferred_element_type=jnp.float32,
        )
    total = jnp.sum(sums, axis=1, keepdims=True)
    mixed_ref[0] = acc / total
    log_ref[0] = jnp.broadcast_to(row_max * score_scale + jnp.log(total), (heads, width))


def suffix_partials(queries, keys, values, lengths, slots, score_scale):
    count, heads, width = queries.shape
    kv_count = keys.shape[2]
    rows = keys.shape[1] * kv_count
    keys = keys.reshape(count, rows, width)
    values = values.reshape(count, rows, width)

    def by_slot(i, slot_ref, length_ref):
        return (lax.rem(slot_ref[i], count), 0, 0)

    def by_request(i, slot_ref, length_ref):
        return (i, 0, 0)

    return pl.pallas_call(
        functools.partial(suffix_kernel, kv_count=kv_count, score_scale=score_scale),
        grid_spec=pltpu.PrefetchScalarGridSpec(
            num_scalar_prefetch=2,
            grid=(count,),
            in_specs=[
                pl.BlockSpec((1, heads, width), by_request),
                pl.BlockSpec((1, rows, width), by_slot),
                pl.BlockSpec((1, rows, width), by_slot),
            ],
            out_specs=[
                pl.BlockSpec((1, heads, width), by_request),
                pl.BlockSpec((1, heads, width), by_request),
            ],
            scratch_shapes=[pltpu.VMEM((heads, rows), jnp.float32)],
        ),
        out_shape=[jax.ShapeDtypeStruct((count, heads, width), jnp.float32)] * 2,
        compiler_params=pltpu.CompilerParams(vmem_limit_bytes=VMEM_BYTES),
        cost_estimate=pl.CostEstimate(
            flops=4 * count * heads * rows * width,
            bytes_accessed=4 * count * rows * width,
            transcendentals=count * heads * rows,
        ),
        name="suffix_attention",
    )(slots, lengths, queries, keys, values)


def prefix_kernel(q_ref, k0_ref, v0_ref, k1_ref, v1_ref, out_ref, score_ref, *, per_dest, score_scale):
    width = q_ref.shape[1]
    tiles = q_ref.shape[0] // ROW_TILE
    dests = ROW_TILE // per_dest
    keys, values = (k0_ref, k1_ref), (v0_ref, v1_ref)
    units = [(tile, block) for tile in range(tiles) for block in range(2)]
    lane = lax.broadcasted_iota(jnp.int32, (per_dest, width), 1)
    row = lax.broadcasted_iota(jnp.int32, (per_dest, width), 0)
    diagonal = lane == row

    def score(unit, slot):
        tile, block = unit
        score_ref[slot] = lax.dot_general(
            q_ref[tile * ROW_TILE : (tile + 1) * ROW_TILE],
            keys[block][...],
            NT,
            preferred_element_type=jnp.float32,
        )

    score(units[0], 0)
    held = None
    for step, (tile, block) in enumerate(units):
        if step + 1 < len(units):
            score(units[step + 1], (step + 1) % 2)
        scores = score_ref[step % 2]
        row_max = jnp.max(scores, axis=1, keepdims=True)
        terms = jnp.exp((scores - row_max) * score_scale)
        total = jnp.sum(terms, axis=1, keepdims=True)
        acc = jnp.dot(
            terms.astype(jnp.bfloat16), values[block][...], preferred_element_type=jnp.float32
        )
        if block == 0:
            held = (row_max, total, acc)
            continue
        max0, total0, acc0 = held
        top = jnp.maximum(max0, row_max)
        weight0 = jnp.exp((max0 - top) * score_scale)
        weight1 = jnp.exp((row_max - top) * score_scale)
        joined = weight0 * total0 + weight1 * total
        mixed = (weight0 * acc0 + weight1 * acc) / joined
        logs = jnp.broadcast_to(top * score_scale + jnp.log(joined), (ROW_TILE, width))
        for k in range(dests):
            rows = slice(k * per_dest, (k + 1) * per_dest)
            dest = tile * dests + k
            out_ref[dest, :per_dest] = mixed[rows]
            line = jnp.sum(jnp.where(diagonal, logs[rows], 0.0), axis=0, keepdims=True)
            out_ref[dest, per_dest:] = jnp.broadcast_to(line, (LOG_ROWS, width))


def prefix_partials(rows_q, keys, values, far_keys, far_values, per_dest, score_scale):
    rows, width = rows_q.shape
    length = keys.shape[0]
    step_rows = min(STEP_ROWS, rows)
    dests = step_rows // per_dest

    def whole(i):
        return (0, 0)

    return pl.pallas_call(
        functools.partial(prefix_kernel, per_dest=per_dest, score_scale=score_scale),
        grid=(rows // step_rows,),
        in_specs=[pl.BlockSpec((step_rows, width), lambda i: (i, 0))]
        + [pl.BlockSpec((length, width), whole)] * 4,
        out_specs=pl.BlockSpec((dests, per_dest + LOG_ROWS, width), lambda i: (i, 0, 0)),
        out_shape=jax.ShapeDtypeStruct((rows // per_dest, per_dest + LOG_ROWS, width), jnp.float32),
        scratch_shapes=[pltpu.VMEM((2, ROW_TILE, length), jnp.float32)],
        compiler_params=pltpu.CompilerParams(vmem_limit_bytes=VMEM_BYTES),
        cost_estimate=pl.CostEstimate(
            flops=8 * rows * length * width,
            bytes_accessed=8 * length * width + 6 * rows * width,
            transcendentals=2 * rows * length,
        ),
        name="prefix_attention",
    )(rows_q, keys, values, far_keys, far_values)


def join_kernel(got_ref, suf_ref, suf_log_ref, out_ref, log_ref, *, kv_count):
    count, heads, width = out_ref.shape
    group = heads // kv_count
    per_dest = count * group
    parts = got_ref.shape[0] // kv_count
    lane = lax.broadcasted_iota(jnp.int32, (per_dest, width), 1)
    row = lax.broadcasted_iota(jnp.int32, (per_dest, width), 0)
    diagonal = lane == row
    lines = [jnp.zeros((1, width), jnp.float32) for _ in range(count)]
    for g in range(kv_count):
        heads_of = slice(g * group, (g + 1) * group)
        suf_log = jnp.concatenate([suf_log_ref[r, heads_of] for r in range(count)], axis=0)
        suf_mixed = jnp.concatenate([suf_ref[r, heads_of] for r in range(count)], axis=0)
        logs = []
        top = suf_log
        for s in range(parts):
            line = got_ref[s * kv_count + g, per_dest : per_dest + 1]
            column = jnp.sum(jnp.where(diagonal, line, 0.0), axis=1, keepdims=True)
            logs.append(jnp.broadcast_to(column, (per_dest, width)))
            top = jnp.maximum(top, logs[-1])
        weight = jnp.exp(suf_log - top)
        acc = weight * suf_mixed
        total = weight
        for s in range(parts):
            weight = jnp.exp(logs[s] - top)
            acc = acc + weight * got_ref[s * kv_count + g, :per_dest]
            total = total + weight
        acc = acc / total
        logged = top + jnp.log(total)
        for r in range(count):
            rows = slice(r * group, (r + 1) * group)
            out_ref[r, heads_of] = acc[rows]
            place = lane[:group] == row[:group] + g * group
            lines[r] = lines[r] + jnp.sum(jnp.where(place, logged[rows], 0.0), axis=0, keepdims=True)
    for r in range(count):
        log_ref[r : r + 1] = lines[r][:, :heads]


def per_device(
    queries, prefix_keys, prefix_values, suffix_keys, suffix_values, suffix_lengths, slot_map
):
    count, heads, width = queries.shape
    kv_count = suffix_keys.shape[2]
    group = heads // kv_count
    score_scale = 1.0 / math.sqrt(width)
    keys = prefix_keys[:, 0, :]
    values = prefix_values[:, 0, :]
    swap = [(i, lax.axis_size("rep") - 1 - i) for i in range(lax.axis_size("rep"))]
    far_keys = lax.ppermute(keys, "rep", swap)
    far_values = lax.ppermute(values, "rep", swap)
    by_group = queries.reshape(count, kv_count, group, width).transpose(1, 0, 2, 3)
    sent = jnp.broadcast_to(
        by_group[None], (lax.axis_size("seq"), kv_count, count, group, width)
    ).reshape(-1, count * group, width)
    got_q = lax.all_to_all(sent, ("seq", "head"), split_axis=0, concat_axis=0, tiled=True)
    suf_mixed, suf_log = suffix_partials(
        queries, suffix_keys, suffix_values, suffix_lengths, slot_map, score_scale
    )
    partials = prefix_partials(
        got_q.reshape(-1, width), keys, values, far_keys, far_values, count * group, score_scale
    )
    got = lax.all_to_all(partials, ("seq", "head"), split_axis=0, concat_axis=0, tiled=True)
    return pl.pallas_call(
        functools.partial(join_kernel, kv_count=kv_count),
        in_specs=[pl.BlockSpec(memory_space=pltpu.VMEM)] * 3,
        out_specs=[pl.BlockSpec(memory_space=pltpu.VMEM)] * 2,
        out_shape=[
            jax.ShapeDtypeStruct((count, heads, width), jnp.float32),
            jax.ShapeDtypeStruct((count, heads), jnp.float32),
        ],
        compiler_params=pltpu.CompilerParams(vmem_limit_bytes=VMEM_BYTES),
        name="join_partials",
    )(got, suf_mixed, suf_log)


def solution(mesh):
    by_request = P(("seq", "head", "rep"))
    by_block = P(("seq", "rep"), "head", None)
    placed = (by_request, by_block, by_block, by_request, by_request, by_request, by_request)
    return jax.shard_map(
        per_device,
        mesh=mesh,
        in_specs=placed,
        out_specs=(by_request, by_request),
        check_vma=False,
    )
```

time: 140 us -> 39.1 us (0.28)
  waiting for transfers between devices: 78 us -> 2.73 us
  matrix products: 16.4 us -> 0 us
  blocking collectives: 0 us -> 15.9 us
  between operations: 14.2 us -> 0.71 us
  Pallas kernels: 0 us -> 10.2 us
  starting transfers between devices: 13.6 us -> 4.14 us
  other arithmetic: 6.91 us -> 0 us
  local copies, waits for them, and re-layouts: 9.72 us -> 5.06 us
    all_gather x1 -> x0, waiting for transfers between devices: 58.1 us -> none  [per_device(): lax.all_gather(queries, ('seq', 'head', 'rep'), axis=0, tiled=True)]
    all_to_all x4 -> x1, waiting for transfers between devices: 19.3 us -> 2.72 us  [per_device(): lax.all_to_all(partials, ('seq', 'head'), split_axis=0, concat_axis=0, ti...]
    dot_general x6 -> x0, matrix products: 16.4 us -> none  [the longest x2 6.06 us: softmax_rows(): jnp.dot(weights, local_values, preferred_element_type=jnp.float32)]
    all_to_all x0 -> x1, blocking collectives: none -> 15.9 us  [per_device(): lax.all_to_all(sent, ('seq', 'head'), split_axis=0, concat_axis=0, tiled=...]
    pallas_call x0 -> x3, Pallas kernels: none -> 10.2 us  [the longest x1 5.57 us: suffix_partials(): pl.pallas_call(functools.partial(suffix_kernel, kv_count=kv_count, score_...]
    all_to_all x4 -> x1, starting transfers between devices: 13.6 us -> 3.54 us  [per_device(): lax.all_to_all(partials, ('seq', 'head'), split_axis=0, concat_axis=0, ti...]
    while x8 -> x0, local copies, waits for them, and re-layouts: 3.87 us -> none
    unnamed x6 -> x12, local copies, waits for them, and re-layouts: 0.77 us -> 4.28 us
  transfers between devices with their start and end apart: 5 -> 3, of which waited for: 5 -> 1; matrix products, arithmetic and copies ran while one was open for 9% -> 2% of each run, Pallas kernels for 0% -> 14%
where the time goes in v1:
time: 39.1 us; the launch traced here: 38.7 us
  blocking collectives  15.9 us (41%)
  Pallas kernels  10.2 us (26%)
  local copies, waits for them, and re-layouts  5.06 us (13%)
  starting transfers between devices  4.14 us (11%)
  waiting for transfers between devices  2.73 us (7%)
  between operations  0.71 us (2%)
    all_to_all x1, blocking collectives, per_device(): lax.all_to_all(sent, ('seq', 'head'), split_axis=0, concat_axis=0, tiled=...  15.9 us
    pallas_call x1, Pallas kernels, suffix_partials(): pl.pallas_call(functools.partial(suffix_kernel, kv_count=kv_count, score_...  5.57 us
    unnamed x12, local copies, waits for them, and re-layouts  4.28 us
    pallas_call x1, Pallas kernels, prefix_partials(): pl.pallas_call(functools.partial(prefix_kernel, per_dest=per_dest, score_...  3.77 us
    all_to_all x1, starting transfers between devices, per_device(): lax.all_to_all(partials, ('seq', 'head'), split_axis=0, concat_axis=0, ti...  3.54 us
    all_to_all x1, waiting for transfers between devices, per_device(): lax.all_to_all(partials, ('seq', 'head'), split_axis=0, concat_axis=0, ti...  2.72 us
    pallas_call x1, Pallas kernels, per_device(): pl.pallas_call(functools.partial(join_kernel, kv_count=kv_count), in_spec...  0.83 us
  transfers between devices with their start and end apart: 3, of which 1 were waited for; matrix products, arithmetic and copies ran while one was open for 2% of the time, Pallas kernels for 14%

profile of v1, /device:TPU:0, one launch (start us, length us, event | category | flops | bytes accessed | tf_op | source)
XLA Modules:
  0.0 38.7 jit_solution(2995712690272490143)
XLA Ops:
  0.6 0.0 copy-start.1
  0.6 0.0 copy-start.3
  0.6 0.0 copy-start.2
  0.7 0.5 %collective-permute-start = (bf16[2048,128]{1,0:T(8,128)(2,1)}, bf16[2048,128]{1,0:T(8,128)(2,1)S(1)}, u32[]{:S(2)}, u32[]{:S(2)}) collective-permute-start(bf16[2048,128]{1,0:T(8,128)(2,1)} %bitcast.12), channel_id=1, source_target_pairs={{0,1},{1,0},{2,3},{3,2},{4,5},{5,4},{6,7},{7,6},{8,9},{9,8},{10,11... | collective-permute-start | bytes 1572872 | tf_op jit(solution)/shard_map/ppermute | solution.py:217
  1.2 0.1 collective-permute-start.1
  1.3 0.8 %copy.9 = bf16[4,2,16,128]{3,2,1,0:T(8,128)(2,1)S(1)} copy(bf16[4,2,16,128]{3,2,0,1:T(8,128)(2,1)} %bitcast.10) | data formatting | bytes 65536 | tf_op jit(solution)/shard_map/transpose | solution.py:219
  2.0 15.9 %all_to_all.10 = bf16[16,32,128]{2,1,0:T(8,128)(2,1)S(1)} all-to-all(bf16[16,32,128]{2,1,0:T(8,128)(2,1)S(1)} %bitcast.17), channel_id=1, replica_groups=mesh['seq'=4,'head'=4,'rep'=2] {'seq','head'}, dimensions={0} | all-to-all | bytes 262144 | tf_op jit(solution)/shard_map/all_to_all | solution.py:223
  17.9 0.0 collective-permute-done.k1_ref
  17.9 0.0 collective-permute-done.1.v1_ref
  17.9 0.0 copy-start.4
  17.9 1.0 %copy-done.4 = bf16[2048,1,128]{2,0,1:T(8,128)(2,1)S(1)} copy-done((bf16[2048,1,128]{2,0,1:T(8,128)(2,1)S(1)}, bf16[2048,1,128]{2,0,1:T(8,128)(2,1)}, u32[]{:S(2)}) %copy-start.4) | copy-done | bytes 524312
  19.0 0.0 copy-start.5
  19.0 1.0 %copy-done.5 = bf16[2048,1,128]{2,0,1:T(8,128)(2,1)S(1)} copy-done((bf16[2048,1,128]{2,0,1:T(8,128)(2,1)S(1)}, bf16[2048,1,128]{2,0,1:T(8,128)(2,1)}, u32[]{:S(2)}) %copy-start.5) | copy-done | bytes 524312
  20.0 3.8 %prefix_attention.1 = f32[16,40,128]{2,1,0:T(8,128)} custom-call(bf16[512,128]{1,0:T(8,128)(2,1)S(1)} %bitcast.11, bf16[2048,128]{1,0:T(8,128)(2,1)S(1)} %bitcast.13, bf16[2048,128]{1,0:T(8,128)(2,1)S(1)} %bitcast.15, bf16[2048,128]{1,0:T(8,128)(2,1)S(1)} %collective-permute-done.k1_ref, bf16[2048,128]{1,0:T(8,128)(2,1)S(1)} %collective-permute-done.1.v1_ref), custom_call_target="tpu_custom_call" | custom-call | flops 1073741824 | bytes 2490368 | tf_op jit(solution)/shard_map/prefix_attention/pallas_call | solution.py:151
  23.8 3.5 %all-to-all-start.1 = ((f32[16,40,128]{2,1,0:T(8,128)}), f32[16,40,128]{2,1,0:T(8,128)S(1)}, u32[]{:S(2)}, u32[]{:S(2)}) async-start(f32[16,40,128]{2,1,0:T(8,128)} %prefix_attention.1), calls=%async_computation.1 | async-start | bytes 655360 | tf_op jit(solution)/shard_map/all_to_all | solution.py:230
  27.4 0.0 copy-done.1
  27.4 0.0 copy-done.3
  27.4 0.0 copy-done.2
  27.4 0.0 copy-start
  27.4 2.2 %copy-done = bf16[2,2048,4,128]{3,2,1,0:T(4,128)(2,1)S(1)} copy-done((bf16[2,2048,4,128]{3,2,1,0:T(4,128)(2,1)S(1)}, bf16[2,2048,4,128]{3,2,1,0:T(4,128)(2,1)}, u32[]{:S(2)}) %copy-start) | copy-done | bytes 4194328
  29.6 5.6 %suffix_attention.1 = (f32[2,64,128]{2,1,0:T(8,128)S(1)}, f32[2,64,128]{2,1,0:T(8,128)S(1)}) custom-call(s32[2]{0:T(128)S(1)} %copy-done.2, s32[2]{0:T(128)S(1)} %copy-done.3, bf16[2,64,128]{2,1,0:T(8,128)(2,1)S(1)} %copy-done.1, bf16[2,8192,128]{2,1,0:T(8,128)(2,1)S(1)} %bitcast.9, bf16[2,8192,128]{2,1,0:T(8,128)(2,1)} %bitcast.16), custom_call_target="tpu_custom_call" | custom-call | flops 536870912 | bytes 8388608 | tf_op jit(solution)/shard_map/suffix_attention/pallas_call | solution.py:66
  35.1 2.7 %all-to-all-done.1.got_ref = f32[16,40,128]{2,1,0:T(8,128)S(1)} async-done(((f32[16,40,128]{2,1,0:T(8,128)}), f32[16,40,128]{2,1,0:T(8,128)S(1)}, u32[]{:S(2)}, u32[]{:S(2)}) %all-to-all-start.1) | async-done | bytes 327712 | tf_op jit(solution)/shard_map/all_to_all | solution.py:230
  37.9 0.8 %join_partials.1 = (f32[2,64,128]{2,1,0:T(8,128)}, f32[2,64]{1,0:T(2,128)}) custom-call(f32[16,40,128]{2,1,0:T(8,128)S(1)} %all-to-all-done.1.got_ref, f32[2,64,128]{2,1,0:T(8,128)S(1)} %get-tuple-element.4.suf_ref, f32[2,64,128]{2,1,0:T(8,128)S(1)} %get-tuple-element.5.suf_log_ref), custom_call_target="tpu_custom_call" | custom-call | tf_op jit(solution)/shard_map/join_partials/pallas_call | solution.py:231
  (1 shorter events, 0.0 us)
Async XLA Ops:
  0.6 26.7 %copy-start.1 = (bf16[2,64,128]{2,1,0:T(8,128)(2,1)S(1)}, bf16[2,64,128]{2,1,0:T(8,128)(2,1)}, u32[]{:S(2)}) copy-start(bf16[2,64,128]{2,1,0:T(8,128)(2,1)} %q_ref.1) | copy-start | bytes 98308
  0.6 26.7 %copy-start.3 = (s32[2]{0:T(128)S(1)}, s32[2]{0:T(128)}, u32[]{:S(2)}) copy-start(s32[2]{0:T(128)} %length_ref.1) | copy-start | bytes 28
  0.6 26.7 %copy-start.2 = (s32[2]{0:T(128)S(1)}, s32[2]{0:T(128)}, u32[]{:S(2)}) copy-start(s32[2]{0:T(128)} %slot_ref.1) | copy-start | bytes 28
  0.7 17.3 %collective-permute-start = (bf16[2048,128]{1,0:T(8,128)(2,1)}, bf16[2048,128]{1,0:T(8,128)(2,1)S(1)}, u32[]{:S(2)}, u32[]{:S(2)}) collective-permute-start(bf16[2048,128]{1,0:T(8,128)(2,1)} %bitcast.12), channel_id=1, source_target_pairs={{0,1},{1,0},{2,3},{3,2},{4,5},{5,4},{6,7},{7,6},{8,9},{9,8},{10,11... | collective-permute-start | bytes 1572872 | tf_op jit(solution)/shard_map/ppermute | solution.py:217
  1.2 16.8 %collective-permute-start.1 = (bf16[2048,128]{1,0:T(8,128)(2,1)}, bf16[2048,128]{1,0:T(8,128)(2,1)S(1)}, u32[]{:S(2)}, u32[]{:S(2)}) collective-permute-start(bf16[2048,128]{1,0:T(8,128)(2,1)} %bitcast.14), channel_id=1, source_target_pairs={{0,1},{1,0},{2,3},{3,2},{4,5},{5,4},{6,7},{7,6},{8,9},{9,8},{10,11... | collective-permute-start | bytes 1572872 | tf_op jit(solution)/shard_map/ppermute | solution.py:218
  17.9 1.0 %copy-start.4 = (bf16[2048,1,128]{2,0,1:T(8,128)(2,1)S(1)}, bf16[2048,1,128]{2,0,1:T(8,128)(2,1)}, u32[]{:S(2)}) copy-start(bf16[2048,1,128]{2,0,1:T(8,128)(2,1)} %param.8) | copy-start | bytes 1572868
  19.0 1.0 %copy-start.5 = (bf16[2048,1,128]{2,0,1:T(8,128)(2,1)S(1)}, bf16[2048,1,128]{2,0,1:T(8,128)(2,1)}, u32[]{:S(2)}) copy-start(bf16[2048,1,128]{2,0,1:T(8,128)(2,1)} %param.9) | copy-start | bytes 1572868
  23.8 14.1 %all-to-all-start.1 = ((f32[16,40,128]{2,1,0:T(8,128)}), f32[16,40,128]{2,1,0:T(8,128)S(1)}, u32[]{:S(2)}, u32[]{:S(2)}) async-start(f32[16,40,128]{2,1,0:T(8,128)} %prefix_attention.1), calls=%async_computation.1 | async-start | bytes 655360 | tf_op jit(solution)/shard_map/all_to_all | solution.py:230
  27.4 2.2 %copy-start = (bf16[2,2048,4,128]{3,2,1,0:T(4,128)(2,1)S(1)}, bf16[2,2048,4,128]{3,2,1,0:T(4,128)(2,1)}, u32[]{:S(2)}) copy-start(bf16[2,2048,4,128]{3,2,1,0:T(4,128)(2,1)} %param.10) | copy-start | bytes 12582916

commit v2 on v1

v2 whole, which is shorter than its diff:
```python
import functools
import math

import jax
import jax.numpy as jnp
from jax import lax
from jax.experimental import pallas as pl
from jax.experimental.pallas import tpu as pltpu
from jax.sharding import PartitionSpec as P

ROW_TILE = 128
CALL_PIECES = 16
SUF_CHUNK = 1024
SUF_COPIES = 4
LOG_ROWS = 8
NT = (((1,), (1,)), ((), ()))
PREFIX_VMEM = 14 * 1024 * 1024
SUFFIX_VMEM = 58 * 1024 * 1024
SMALL_VMEM = 8 * 1024 * 1024
IN_VMEM = pl.BlockSpec(memory_space=pltpu.VMEM)
IN_SMEM = pl.BlockSpec(memory_space=pltpu.SMEM)
IN_HBM = pl.BlockSpec(memory_space=pltpu.HBM)


def split_kernel(q_ref, *piece_refs):
    count = q_ref.shape[0]
    group = q_ref.shape[1] // len(piece_refs)
    own = lax.axis_index("head")
    for d, piece_ref in enumerate(piece_refs):
        begin = pl.multiple_of((own ^ d) * group, group)
        for r in range(count):
            piece_ref[r * group : (r + 1) * group] = q_ref[r, pl.ds(begin, group)]


def split_queries(queries, kv_count):
    count, heads, width = queries.shape
    piece = jax.ShapeDtypeStruct((count * heads // kv_count, width), queries.dtype)
    return pl.pallas_call(
        split_kernel,
        in_specs=[IN_VMEM],
        out_specs=[IN_VMEM] * kv_count,
        out_shape=[piece] * kv_count,
        compiler_params=pltpu.CompilerParams(vmem_limit_bytes=SMALL_VMEM),
        name="split_queries",
    )(queries)


def suffix_kernel(
    slot_ref, length_ref, q_ref, k_hbm, v_hbm, mixed_ref, log_ref, k_buf, v_buf, score_ref, sems, *, kv_count, score_scale
):
    count, heads, width = q_ref.shape
    rows = k_hbm.shape[1]
    copy_rows = rows // SUF_COPIES
    copies = {}
    for r in range(count):
        slot = lax.rem(slot_ref[r], count)
        for which, (source, target) in enumerate(((k_hbm, k_buf), (v_hbm, v_buf))):
            for c in range(SUF_COPIES):
                part = pl.ds(c * copy_rows, copy_rows)
                copies[r, which, c] = pltpu.make_async_copy(
                    source.at[slot, part], target.at[r, part], sems.at[r, which, c]
                )
                copies[r, which, c].start()
    lane = lax.broadcasted_iota(jnp.int32, (heads, SUF_CHUNK), 1)
    group = lax.broadcasted_iota(jnp.int32, (heads, SUF_CHUNK), 0) // (heads // kv_count)
    own_head = (lane % kv_count) == group
    for r in range(count):
        limit = length_ref[r] * kv_count
        query = q_ref[r]
        peak = jnp.full((heads, SUF_CHUNK), -1e30, jnp.float32)
        for begin in range(0, rows, SUF_CHUNK):
            if begin % copy_rows == 0:
                copies[r, 0, begin // copy_rows].wait()
            part = lax.dot_general(
                query, k_buf[r, begin : begin + SUF_CHUNK], NT, preferred_element_type=jnp.float32
            )
            part = jnp.where(own_head & (lane < limit - begin), part, -1e30)
            score_ref[:, begin : begin + SUF_CHUNK] = part
            peak = jnp.maximum(peak, part)
        row_max = jnp.max(peak, axis=1, keepdims=True)
        sums = jnp.zeros((heads, SUF_CHUNK), jnp.float32)
        acc = jnp.zeros((heads, width), jnp.float32)
        for begin in range(0, rows, SUF_CHUNK):
            if begin % copy_rows == 0:
                copies[r, 1, begin // copy_rows].wait()
            terms = jnp.exp((score_ref[:, begin : begin + SUF_CHUNK] - row_max) * score_scale)
            sums = sums + terms
            acc = acc + jnp.dot(
                terms.astype(jnp.bfloat16),
                v_buf[r, begin : begin + SUF_CHUNK],
                preferred_element_type=jnp.float32,
            )
        total = jnp.sum(sums, axis=1, keepdims=True)
        mixed_ref[r] = acc / total
        log_ref[r] = jnp.broadcast_to(row_max * score_scale + jnp.log(total), (heads, width))


def suffix_partials(queries, keys, values, lengths, slots, score_scale):
    count, heads, width = queries.shape
    kv_count = keys.shape[2]
    rows = keys.shape[1] * kv_count
    return pl.pallas_call(
        functools.partial(suffix_kernel, kv_count=kv_count, score_scale=score_scale),
        in_specs=[IN_SMEM, IN_SMEM, IN_VMEM, IN_HBM, IN_HBM],
        out_specs=[IN_VMEM, IN_VMEM],
        out_shape=[jax.ShapeDtypeStruct((count, heads, width), jnp.float32)] * 2,
        scratch_shapes=[
            pltpu.VMEM((count, rows, width), keys.dtype),
            pltpu.VMEM((count, rows, width), values.dtype),
            pltpu.VMEM((heads, rows), jnp.float32),
            pltpu.SemaphoreType.DMA((count, 2, SUF_COPIES)),
        ],
        compiler_params=pltpu.CompilerParams(vmem_limit_bytes=SUFFIX_VMEM),
        cost_estimate=pl.CostEstimate(
            flops=4 * count * heads * rows * width,
            bytes_accessed=4 * count * rows * width,
            transcendentals=count * heads * rows,
        ),
        name="suffix_attention",
    )(slots, lengths, queries, keys.reshape(count, rows, width), values.reshape(count, rows, width))


def prefix_kernel(*refs, pieces, score_scale):
    q_refs, (k0_ref, v0_ref, k1_ref, v1_ref) = refs[:pieces], refs[pieces : pieces + 4]
    out_refs, score_ref = refs[pieces + 4 : -1], refs[-1]
    per_dest, width = q_refs[0].shape
    per_tile = ROW_TILE // per_dest
    keys, values = (k0_ref, k1_ref), (v0_ref, v1_ref)
    units = [(tile, block) for tile in range(pieces // per_tile) for block in range(2)]
    lane = lax.broadcasted_iota(jnp.int32, (per_dest, width), 1)
    row = lax.broadcasted_iota(jnp.int32, (per_dest, width), 0)
    diagonal = lane == row

    def score(unit, slot):
        tile, block = unit
        query = jnp.concatenate(
            [q_refs[tile * per_tile + k][...] for k in range(per_tile)], axis=0
        )
        score_ref[slot] = lax.dot_general(
            query, keys[block][...], NT, preferred_element_type=jnp.float32
        )

    score(units[0], 0)
    held = None
    for step, (tile, block) in enumerate(units):
        if step + 1 < len(units):
            score(units[step + 1], (step + 1) % 2)
        scores = score_ref[step % 2]
        row_max = jnp.max(scores, axis=1, keepdims=True)
        terms = jnp.exp((scores - row_max) * score_scale)
        total = jnp.sum(terms, axis=1, keepdims=True)
        acc = jnp.dot(
            terms.astype(jnp.bfloat16), values[block][...], preferred_element_type=jnp.float32
        )
        if block == 0:
            held = (row_max, total, acc)
            continue
        max0, total0, acc0 = held
        top = jnp.maximum(max0, row_max)
        weight0 = jnp.exp((max0 - top) * score_scale)
        weight1 = jnp.exp((row_max - top) * score_scale)
        joined = weight0 * total0 + weight1 * total
        mixed = (weight0 * acc0 + weight1 * acc) / joined
        logs = jnp.broadcast_to(top * score_scale + jnp.log(joined), (ROW_TILE, width))
        for k in range(per_tile):
            rows = slice(k * per_dest, (k + 1) * per_dest)
            out_ref = out_refs[tile * per_tile + k]
            out_ref[:per_dest] = mixed[rows]
            line = jnp.sum(jnp.where(diagonal, logs[rows], 0.0), axis=0, keepdims=True)
            out_ref[per_dest:] = jnp.broadcast_to(line, (LOG_ROWS, width))


def prefix_partials(pieces_q, keys, values, far_keys, far_values, score_scale):
    pieces = len(pieces_q)
    per_dest, width = pieces_q[0].shape
    length = keys.shape[0]
    rows = pieces * per_dest
    piece = jax.ShapeDtypeStruct((per_dest + LOG_ROWS, width), jnp.float32)
    return pl.pallas_call(
        functools.partial(prefix_kernel, pieces=pieces, score_scale=score_scale),
        in_specs=[IN_VMEM] * (pieces + 4),
        out_specs=[IN_VMEM] * pieces,
        out_shape=[piece] * pieces,
        scratch_shapes=[pltpu.VMEM((2, ROW_TILE, length), jnp.float32)],
        compiler_params=pltpu.CompilerParams(vmem_limit_bytes=PREFIX_VMEM),
        cost_estimate=pl.CostEstimate(
            flops=8 * rows * length * width,
            bytes_accessed=8 * length * width + 6 * rows * width,
            transcendentals=2 * rows * length,
        ),
        name="prefix_attention",
    )(*pieces_q, keys, values, far_keys, far_values)


def join_kernel(*refs, kv_count):
    got_refs = refs[:-4]
    suf_ref, suf_log_ref, out_ref, log_ref = refs[-4:]
    count, heads, width = out_ref.shape
    group = heads // kv_count
    per_dest = count * group
    parts = len(got_refs) // kv_count
    own = lax.axis_index("head")
    lane = lax.broadcasted_iota(jnp.int32, (per_dest, width), 1)
    row = lax.broadcasted_iota(jnp.int32, (per_dest, width), 0)
    diagonal = lane == row
    lines = [jnp.zeros((1, width), jnp.float32) for _ in range(count)]
    for d in range(kv_count):
        begin = pl.multiple_of((own ^ d) * group, group)
        heads_of = pl.ds(begin, group)
        suf_log = jnp.concatenate([suf_log_ref[r, heads_of] for r in range(count)], axis=0)
        suf_mixed = jnp.concatenate([suf_ref[r, heads_of] for r in range(count)], axis=0)
        logs = []
        top = suf_log
        for s in range(parts):
            line = got_refs[s * kv_count + d][per_dest : per_dest + 1]
            column = jnp.sum(jnp.where(diagonal, line, 0.0), axis=1, keepdims=True)
            logs.append(jnp.broadcast_to(column, (per_dest, width)))
            top = jnp.maximum(top, logs[-1])
        weight = jnp.exp(suf_log - top)
        acc = weight * suf_mixed
        total = weight
        for s in range(parts):
            weight = jnp.exp(logs[s] - top)
            acc = acc + weight * got_refs[s * kv_count + d][:per_dest]
            total = total + weight
        acc = acc / total
        logged = top + jnp.log(total)
        for r in range(count):
            rows = slice(r * group, (r + 1) * group)
            out_ref[r, heads_of] = acc[rows]
            place = lane[:group] == row[:group] + begin
            lines[r] = lines[r] + jnp.sum(jnp.where(place, logged[rows], 0.0), axis=0, keepdims=True)
    for r in range(count):
        log_ref[r : r + 1] = lines[r][:, :heads]


def join_partials(got, suf_mixed, suf_log, kv_count):
    count, heads, width = suf_mixed.shape
    return pl.pallas_call(
        functools.partial(join_kernel, kv_count=kv_count),
        in_specs=[IN_VMEM] * (len(got) + 2),
        out_specs=[IN_VMEM] * 2,
        out_shape=[
            jax.ShapeDtypeStruct((count, heads, width), jnp.float32),
            jax.ShapeDtypeStruct((count, heads), jnp.float32),
        ],
        compiler_params=pltpu.CompilerParams(vmem_limit_bytes=SMALL_VMEM),
        name="join_partials",
    )(*got, suf_mixed, suf_log)


def per_device(
    queries, prefix_keys, prefix_values, suffix_keys, suffix_values, suffix_lengths, slot_map
):
    width = queries.shape[2]
    kv_count = suffix_keys.shape[2]
    score_scale = 1.0 / math.sqrt(width)
    seq_devices, head_devices = lax.axis_size("seq"), lax.axis_size("head")
    offsets = [(s, h) for s in range(seq_devices) for h in range(head_devices)]

    def cross(array, offset):
        if offset == (0, 0):
            return array
        step = offset[0] * head_devices + offset[1]
        pairs = [(i, i ^ step) for i in range(seq_devices * head_devices)]
        return lax.ppermute(array, ("seq", "head"), pairs)

    sent = split_queries(queries, kv_count)
    got_q = [cross(sent[h], (s, h)) for s, h in offsets]
    keys = prefix_keys[:, 0, :]
    values = prefix_values[:, 0, :]
    far_keys = lax.ppermute(keys, "rep", [(0, 1), (1, 0)])
    far_values = lax.ppermute(values, "rep", [(0, 1), (1, 0)])
    suf_mixed, suf_log = suffix_partials(
        queries, suffix_keys, suffix_values, suffix_lengths, slot_map, score_scale
    )
    got = []
    for begin in range(0, len(offsets), CALL_PIECES):
        some = slice(begin, begin + CALL_PIECES)
        partials = prefix_partials(got_q[some], keys, values, far_keys, far_values, score_scale)
        got += [cross(part, offset) for part, offset in zip(partials, offsets[some])]
    return join_partials(got, suf_mixed, suf_log, kv_count)


def solution(mesh):
    by_request = P(("seq", "head", "rep"))
    by_block = P(("seq", "rep"), "head", None)
    placed = (by_request, by_block, by_block, by_request, by_request, by_request, by_request)
    return jax.shard_map(
        per_device,
        mesh=mesh,
        in_specs=placed,
        out_specs=(by_request, by_request),
        check_vma=False,
    )
```

time: 39.1 us -> 79.4 us (2.03)
  starting transfers between devices: 4.14 us -> 54.4 us
  blocking collectives: 15.9 us -> 0 us
  waiting for transfers between devices: 2.73 us -> 8.16 us
  Pallas kernels: 10.2 us -> 11.1 us
    ppermute x2 -> x32, starting transfers between devices: 0.6 us -> 54.4 us  [the longest x30 53.8 us: cross(): return lax.ppermute(array, ('seq', 'head'), pairs)]
    all_to_all x1 -> x0, blocking collectives: 15.9 us -> none  [per_device(): lax.all_to_all(sent, ('seq', 'head'), split_axis=0, concat_axis=0, tiled=...]
    ppermute x2 -> x32, waiting for transfers between devices: 0.01 us -> 8.16 us  [the longest x30 8.15 us: cross(): return lax.ppermute(array, ('seq', 'head'), pairs)]
    all_to_all x1 -> x0, starting transfers between devices: 3.54 us -> none  [per_device(): lax.all_to_all(partials, ('seq', 'head'), split_axis=0, concat_axis=0, ti...]
    all_to_all x1 -> x0, waiting for transfers between devices: 2.72 us -> none  [per_device(): lax.all_to_all(partials, ('seq', 'head'), split_axis=0, concat_axis=0, ti...]
    pallas_call x1, Pallas kernels: 5.57 us -> 7.24 us  [suffix_partials(): pl.pallas_call(functools.partial(suffix_kernel, kv_count=kv_count, score_...]
    pallas_call x2 -> x3, Pallas kernels: 4.6 us -> 3.9 us  [the longest x1 3.06 us: prefix_partials(): pl.pallas_call(functools.partial(prefix_kernel, pieces=pieces, score_scal...]
    unnamed x12 -> x10, local copies, waits for them, and re-layouts: 4.28 us -> 4.51 us
  transfers between devices with their start and end apart: 3 -> 32, of which waited for: 1 -> 5; matrix products, arithmetic and copies ran while one was open for 2% -> 0% of each run, Pallas kernels for 14% -> 9%
where the time goes in v2:
time: 79.4 us; the launch traced here: 78.9 us
  starting transfers between devices  54.4 us (69%)
  Pallas kernels  11.1 us (14%)
  waiting for transfers between devices  8.16 us (10%)
  local copies, waits for them, and re-layouts  4.51 us (6%)
    ppermute x30, starting transfers between devices, cross(): return lax.ppermute(array, ('seq', 'head'), pairs)  53.8 us
    ppermute x30, waiting for transfers between devices, cross(): return lax.ppermute(array, ('seq', 'head'), pairs)  8.15 us
    pallas_call x1, Pallas kernels, suffix_partials(): pl.pallas_call(functools.partial(suffix_kernel, kv_count=kv_count, score_...  7.24 us
    unnamed x10, local copies, waits for them, and re-layouts  4.51 us
    pallas_call x1, Pallas kernels, prefix_partials(): pl.pallas_call(functools.partial(prefix_kernel, pieces=pieces, score_scal...  3.06 us
  transfers between devices with their start and end apart: 32, of which 5 were waited for; matrix products, arithmetic and copies ran while one was open for 0% of the time, Pallas kernels for 9%

profile of v2, /device:TPU:0, one launch (start us, length us, event | category | flops | bytes accessed | tf_op | source)
XLA Modules:
  0.0 78.9 jit_solution(10113263817272724206)
XLA Ops:
  2.0 2.9 %collective-permute-start = (bf16[32,128]{1,0:T(8,128)(2,1)S(1)}, bf16[32,128]{1,0:T(8,128)(2,1)S(1)}, u32[]{:S(2)}, u32[]{:S(2)}) collective-permute-start(bf16[32,128]{1,0:T(8,128)(2,1)S(1)} %get-tuple-element.25), channel_id=1, source_target_pairs={{0,2},{2,0},{4,6},{6,4},{8,10},{10,8},{12,14},{14,12},{16,18},{18,... | collective-permute-start | bytes 24584 | tf_op jit(solution)/shard_map/ppermute | solution.py:266
  4.9 1.5 %collective-permute-start.1 = (bf16[32,128]{1,0:T(8,128)(2,1)S(1)}, bf16[32,128]{1,0:T(8,128)(2,1)S(1)}, u32[]{:S(2)}, u32[]{:S(2)}) collective-permute-start(bf16[32,128]{1,0:T(8,128)(2,1)S(1)} %get-tuple-element.26), channel_id=1, source_target_pairs={{0,4},{2,6},{4,0},{6,2},{8,12},{10,14},{12,8},{14,10},{16,20},{18,... | collective-permute-start | bytes 24584 | tf_op jit(solution)/shard_map/ppermute | solution.py:266
  6.4 2.5 %collective-permute-start.10 = (bf16[32,128]{1,0:T(8,128)(2,1)S(1)}, bf16[32,128]{1,0:T(8,128)(2,1)S(1)}, u32[]{:S(2)}, u32[]{:S(2)}) collective-permute-start(bf16[32,128]{1,0:T(8,128)(2,1)S(1)} %get-tuple-element.27), channel_id=1, source_target_pairs={{0,22},{2,20},{4,18},{6,16},{8,30},{10,28},{12,26},{14,24},{16,6},... | collective-permute-start | bytes 24584 | tf_op jit(solution)/shard_map/ppermute | solution.py:266
  8.9 1.7 %collective-permute-start.11 = (bf16[32,128]{1,0:T(8,128)(2,1)S(1)}, bf16[32,128]{1,0:T(8,128)(2,1)S(1)}, u32[]{:S(2)}, u32[]{:S(2)}) collective-permute-start(bf16[32,128]{1,0:T(8,128)(2,1)S(1)} %get-tuple-element.24.refs_0_), channel_id=1, source_target_pairs={{0,24},{2,26},{4,28},{6,30},{8,16},{10,18},{12,20},{14,22},{16,8},... | collective-permute-start | bytes 24584 | tf_op jit(solution)/shard_map/ppermute | solution.py:266
  10.7 3.0 %collective-permute-start.12 = (bf16[32,128]{1,0:T(8,128)(2,1)S(1)}, bf16[32,128]{1,0:T(8,128)(2,1)S(1)}, u32[]{:S(2)}, u32[]{:S(2)}) collective-permute-start(bf16[32,128]{1,0:T(8,128)(2,1)S(1)} %get-tuple-element.25), channel_id=1, source_target_pairs={{0,26},{2,24},{4,30},{6,28},{8,18},{10,16},{12,22},{14,20},{16,10}... | collective-permute-start | bytes 24584 | tf_op jit(solution)/shard_map/ppermute | solution.py:266
  13.7 2.7 %collective-permute-start.13 = (bf16[32,128]{1,0:T(8,128)(2,1)S(1)}, bf16[32,128]{1,0:T(8,128)(2,1)S(1)}, u32[]{:S(2)}, u32[]{:S(2)}) collective-permute-start(bf16[32,128]{1,0:T(8,128)(2,1)S(1)} %get-tuple-element.26), channel_id=1, source_target_pairs={{0,28},{2,30},{4,24},{6,26},{8,20},{10,22},{12,16},{14,18},{16,12}... | collective-permute-start | bytes 24584 | tf_op jit(solution)/shard_map/ppermute | solution.py:266
  16.4 2.0 %collective-permute-start.14 = (bf16[32,128]{1,0:T(8,128)(2,1)S(1)}, bf16[32,128]{1,0:T(8,128)(2,1)S(1)}, u32[]{:S(2)}, u32[]{:S(2)}) collective-permute-start(bf16[32,128]{1,0:T(8,128)(2,1)S(1)} %get-tuple-element.27), channel_id=1, source_target_pairs={{0,30},{2,28},{4,26},{6,24},{8,22},{10,20},{12,18},{14,16},{16,14}... | collective-permute-start | bytes 24584 | tf_op jit(solution)/shard_map/ppermute | solution.py:266
  18.4 2.4 %collective-permute-start.2 = (bf16[32,128]{1,0:T(8,128)(2,1)S(1)}, bf16[32,128]{1,0:T(8,128)(2,1)S(1)}, u32[]{:S(2)}, u32[]{:S(2)}) collective-permute-start(bf16[32,128]{1,0:T(8,128)(2,1)S(1)} %get-tuple-element.27), channel_id=1, source_target_pairs={{0,6},{2,4},{4,2},{6,0},{8,14},{10,12},{12,10},{14,8},{16,22},{18,... | collective-permute-start | bytes 24584 | tf_op jit(solution)/shard_map/ppermute | solution.py:266
  20.9 2.8 %collective-permute-done.14.refs_15_ = bf16[32,128]{1,0:T(8,128)(2,1)S(1)} collective-permute-done((bf16[32,128]{1,0:T(8,128)(2,1)S(1)}, bf16[32,128]{1,0:T(8,128)(2,1)S(1)}, u32[]{:S(2)}, u32[]{:S(2)}) %collective-permute-start.14) | collective-permute-done | bytes 8224 | tf_op jit(solution)/shard_map/ppermute | solution.py:266
  23.7 2.9 %collective-permute-start.5 = (bf16[32,128]{1,0:T(8,128)(2,1)S(1)}, bf16[32,128]{1,0:T(8,128)(2,1)S(1)}, u32[]{:S(2)}, u32[]{:S(2)}) collective-permute-start(bf16[32,128]{1,0:T(8,128)(2,1)S(1)} %get-tuple-element.26), channel_id=1, source_target_pairs={{0,12},{2,14},{4,8},{6,10},{8,4},{10,6},{12,0},{14,2},{16,28},{18,... | collective-permute-start | bytes 24584 | tf_op jit(solution)/shard_map/ppermute | solution.py:266
  28.2 1.9 %collective-permute-start.7 = (bf16[32,128]{1,0:T(8,128)(2,1)S(1)}, bf16[32,128]{1,0:T(8,128)(2,1)S(1)}, u32[]{:S(2)}, u32[]{:S(2)}) collective-permute-start(bf16[32,128]{1,0:T(8,128)(2,1)S(1)} %get-tuple-element.24.refs_0_), channel_id=1, source_target_pairs={{0,16},{2,18},{4,20},{6,22},{8,24},{10,26},{12,28},{14,30},{16,0},... | collective-permute-start | bytes 24584 | tf_op jit(solution)/shard_map/ppermute | solution.py:266
  30.1 1.6 %collective-permute-start.8 = (bf16[32,128]{1,0:T(8,128)(2,1)S(1)}, bf16[32,128]{1,0:T(8,128)(2,1)S(1)}, u32[]{:S(2)}, u32[]{:S(2)}) collective-permute-start(bf16[32,128]{1,0:T(8,128)(2,1)S(1)} %get-tuple-element.25), channel_id=1, source_target_pairs={{0,18},{2,16},{4,22},{6,20},{8,26},{10,24},{12,30},{14,28},{16,2},... | collective-permute-start | bytes 24584 | tf_op jit(solution)/shard_map/ppermute | solution.py:266
  33.0 2.6 %collective-permute-done.8.refs_9_ = bf16[32,128]{1,0:T(8,128)(2,1)S(1)} collective-permute-done((bf16[32,128]{1,0:T(8,128)(2,1)S(1)}, bf16[32,128]{1,0:T(8,128)(2,1)S(1)}, u32[]{:S(2)}, u32[]{:S(2)}) %collective-permute-start.8) | collective-permute-done | bytes 8224 | tf_op jit(solution)/shard_map/ppermute | solution.py:266
  35.6 1.9 %collective-permute-done.9.refs_10_ = bf16[32,128]{1,0:T(8,128)(2,1)S(1)} collective-permute-done((bf16[32,128]{1,0:T(8,128)(2,1)S(1)}, bf16[32,128]{1,0:T(8,128)(2,1)S(1)}, u32[]{:S(2)}, u32[]{:S(2)}) %collective-permute-start.9) | collective-permute-done | bytes 8224 | tf_op jit(solution)/shard_map/ppermute | solution.py:266
  39.5 3.1 %prefix_attention.1 = (f32[40,128]{1,0:T(8,128)S(1)}, f32[40,128]{1,0:T(8,128)S(1)}, f32[40,128]{1,0:T(8,128)S(1)}, f32[40,128]{1,0:T(8,128)S(1)}, f32[40,128]{1...) custom-call(bf16[32,128]{1,0:T(8,128)(2,1)S(1)} %get-tuple-element.2, ...), custom_call_target="tpu_custom_call" | custom-call | flops 1073741824 | bytes 2490368 | tf_op jit(solution)/shard_map/prefix_attention/pallas_call | solution.py:179
  42.6 1.6 %collective-permute-start.17 = (f32[40,128]{1,0:T(8,128)S(1)}, f32[40,128]{1,0:T(8,128)S(1)}, u32[]{:S(2)}, u32[]{:S(2)}) collective-permute-start(f32[40,128]{1,0:T(8,128)S(1)} %get-tuple-element.29), channel_id=1, source_target_pairs={{0,2},{2,0},{4,6},{6,4},{8,10},{10,8},{12,14},{14,12},{16,18},{18,... | collective-permute-start | bytes 61448 | tf_op jit(solution)/shard_map/ppermute | solution.py:266
  46.6 2.6 %collective-permute-start.21 = (f32[40,128]{1,0:T(8,128)S(1)}, f32[40,128]{1,0:T(8,128)S(1)}, u32[]{:S(2)}, u32[]{:S(2)}) collective-permute-start(f32[40,128]{1,0:T(8,128)S(1)} %get-tuple-element.33), channel_id=1, source_target_pairs={{0,10},{2,8},{4,14},{6,12},{8,2},{10,0},{12,6},{14,4},{16,26},{18,... | collective-permute-start | bytes 61448 | tf_op jit(solution)/shard_map/ppermute | solution.py:266
  53.1 2.9 %collective-permute-start.25 = (f32[40,128]{1,0:T(8,128)S(1)}, f32[40,128]{1,0:T(8,128)S(1)}, u32[]{:S(2)}, u32[]{:S(2)}) collective-permute-start(f32[40,128]{1,0:T(8,128)S(1)} %get-tuple-element.37), channel_id=1, source_target_pairs={{0,18},{2,16},{4,22},{6,20},{8,26},{10,24},{12,30},{14,28},{16,2},... | collective-permute-start | bytes 61448 | tf_op jit(solution)/shard_map/ppermute | solution.py:266
  56.9 2.7 %collective-permute-start.27 = (f32[40,128]{1,0:T(8,128)S(1)}, f32[40,128]{1,0:T(8,128)S(1)}, u32[]{:S(2)}, u32[]{:S(2)}) collective-permute-start(f32[40,128]{1,0:T(8,128)S(1)} %get-tuple-element.39), channel_id=1, source_target_pairs={{0,22},{2,20},{4,18},{6,16},{8,30},{10,28},{12,26},{14,24},{16,6},... | collective-permute-start | bytes 61448 | tf_op jit(solution)/shard_map/ppermute | solution.py:266
  59.7 1.6 %collective-permute-start.28 = (f32[40,128]{1,0:T(8,128)S(1)}, f32[40,128]{1,0:T(8,128)S(1)}, u32[]{:S(2)}, u32[]{:S(2)}) collective-permute-start(f32[40,128]{1,0:T(8,128)S(1)} %get-tuple-element.40), channel_id=1, source_target_pairs={{0,24},{2,26},{4,28},{6,30},{8,16},{10,18},{12,20},{14,22},{16,8},... | collective-permute-start | bytes 61448 | tf_op jit(solution)/shard_map/ppermute | solution.py:266
  61.2 3.3 %collective-permute-start.29 = (f32[40,128]{1,0:T(8,128)S(1)}, f32[40,128]{1,0:T(8,128)S(1)}, u32[]{:S(2)}, u32[]{:S(2)}) collective-permute-start(f32[40,128]{1,0:T(8,128)S(1)} %get-tuple-element.41), channel_id=1, source_target_pairs={{0,26},{2,24},{4,30},{6,28},{8,18},{10,16},{12,22},{14,20},{16,10}... | collective-permute-start | bytes 61448 | tf_op jit(solution)/shard_map/ppermute | solution.py:266
  64.5 2.1 %collective-permute-start.30 = (f32[40,128]{1,0:T(8,128)S(1)}, f32[40,128]{1,0:T(8,128)S(1)}, u32[]{:S(2)}, u32[]{:S(2)}) collective-permute-start(f32[40,128]{1,0:T(8,128)S(1)} %get-tuple-element.42), channel_id=1, source_target_pairs={{0,28},{2,30},{4,24},{6,26},{8,20},{10,22},{12,16},{14,18},{16,12}... | collective-permute-start | bytes 61448 | tf_op jit(solution)/shard_map/ppermute | solution.py:266
  66.6 2.5 %collective-permute-start.31 = (f32[40,128]{1,0:T(8,128)S(1)}, f32[40,128]{1,0:T(8,128)S(1)}, u32[]{:S(2)}, u32[]{:S(2)}) collective-permute-start(f32[40,128]{1,0:T(8,128)S(1)} %get-tuple-element.43), channel_id=1, source_target_pairs={{0,30},{2,28},{4,26},{6,24},{8,22},{10,20},{12,18},{14,16},{16,14}... | collective-permute-start | bytes 61448 | tf_op jit(solution)/shard_map/ppermute | solution.py:266
  69.1 7.2 %suffix_attention.1 = (f32[2,64,128]{2,1,0:T(8,128)}, f32[2,64,128]{2,1,0:T(8,128)}) custom-call(s32[2]{0:T(128)} %slot_ref.1, s32[2]{0:T(128)} %length_ref.1, bf16[2,64,128]{2,1,0:T(8,128)(2,1)} %q_ref.3, bf16[2,8192,128]{2,1,0:T(8,128)(2,1)} %bitcast.8, bf16[2,8192,128]{2,1,0:T(8,128)(2,1)} %bitcast.9), custom_call_target="tpu_custom_call" | custom-call | flops 536870912 | bytes 8388608 | tf_op jit(solution)/shard_map/suffix_attention/pallas_call | solution.py:102
  (54 shorter events, 16.1 us)
Async XLA Ops:
  0.6 36.8 %collective-permute-start.15 = (bf16[2048,128]{1,0:T(8,128)(2,1)}, bf16[2048,128]{1,0:T(8,128)(2,1)S(1)}, u32[]{:S(2)}, u32[]{:S(2)}) collective-permute-start(bf16[2048,128]{1,0:T(8,128)(2,1)} %bitcast.4), channel_id=1, source_target_pairs={{0,1},{1,0},{2,3},{3,2},{4,5},{5,4},{6,7},{7,6},{8,9},{9,8},{10,11... | collective-permute-start | bytes 1572872 | tf_op jit(solution)/shard_map/ppermute | solution.py:272
  1.1 36.3 %collective-permute-start.16 = (bf16[2048,128]{1,0:T(8,128)(2,1)}, bf16[2048,128]{1,0:T(8,128)(2,1)S(1)}, u32[]{:S(2)}, u32[]{:S(2)}) collective-permute-start(bf16[2048,128]{1,0:T(8,128)(2,1)} %bitcast.6), channel_id=1, source_target_pairs={{0,1},{1,0},{2,3},{3,2},{4,5},{5,4},{6,7},{7,6},{8,9},{9,8},{10,11... | collective-permute-start | bytes 1572872 | tf_op jit(solution)/shard_map/ppermute | solution.py:273
  2.0 6.9 %collective-permute-start = (bf16[32,128]{1,0:T(8,128)(2,1)S(1)}, bf16[32,128]{1,0:T(8,128)(2,1)S(1)}, u32[]{:S(2)}, u32[]{:S(2)}) collective-permute-start(bf16[32,128]{1,0:T(8,128)(2,1)S(1)} %get-tuple-element.25), channel_id=1, source_target_pairs={{0,2},{2,0},{4,6},{6,4},{8,10},{10,8},{12,14},{14,12},{16,18},{18,... | collective-permute-start | bytes 24584 | tf_op jit(solution)/shard_map/ppermute | solution.py:266
  6.4 7.3 %collective-permute-start.10 = (bf16[32,128]{1,0:T(8,128)(2,1)S(1)}, bf16[32,128]{1,0:T(8,128)(2,1)S(1)}, u32[]{:S(2)}, u32[]{:S(2)}) collective-permute-start(bf16[32,128]{1,0:T(8,128)(2,1)S(1)} %get-tuple-element.27), channel_id=1, source_target_pairs={{0,22},{2,20},{4,18},{6,16},{8,30},{10,28},{12,26},{14,24},{16,6},... | collective-permute-start | bytes 24584 | tf_op jit(solution)/shard_map/ppermute | solution.py:266
  8.9 7.5 %collective-permute-start.11 = (bf16[32,128]{1,0:T(8,128)(2,1)S(1)}, bf16[32,128]{1,0:T(8,128)(2,1)S(1)}, u32[]{:S(2)}, u32[]{:S(2)}) collective-permute-start(bf16[32,128]{1,0:T(8,128)(2,1)S(1)} %get-tuple-element.24.refs_0_), channel_id=1, source_target_pairs={{0,24},{2,26},{4,28},{6,30},{8,16},{10,18},{12,20},{14,22},{16,8},... | collective-permute-start | bytes 24584 | tf_op jit(solution)/shard_map/ppermute | solution.py:266
  10.7 7.7 %collective-permute-start.12 = (bf16[32,128]{1,0:T(8,128)(2,1)S(1)}, bf16[32,128]{1,0:T(8,128)(2,1)S(1)}, u32[]{:S(2)}, u32[]{:S(2)}) collective-permute-start(bf16[32,128]{1,0:T(8,128)(2,1)S(1)} %get-tuple-element.25), channel_id=1, source_target_pairs={{0,26},{2,24},{4,30},{6,28},{8,18},{10,16},{12,22},{14,20},{16,10}... | collective-permute-start | bytes 24584 | tf_op jit(solution)/shard_map/ppermute | solution.py:266
  13.7 7.2 %collective-permute-start.13 = (bf16[32,128]{1,0:T(8,128)(2,1)S(1)}, bf16[32,128]{1,0:T(8,128)(2,1)S(1)}, u32[]{:S(2)}, u32[]{:S(2)}) collective-permute-start(bf16[32,128]{1,0:T(8,128)(2,1)S(1)} %get-tuple-element.26), channel_id=1, source_target_pairs={{0,28},{2,30},{4,24},{6,26},{8,20},{10,22},{12,16},{14,18},{16,12}... | collective-permute-start | bytes 24584 | tf_op jit(solution)/shard_map/ppermute | solution.py:266
  16.4 7.2 %collective-permute-start.14 = (bf16[32,128]{1,0:T(8,128)(2,1)S(1)}, bf16[32,128]{1,0:T(8,128)(2,1)S(1)}, u32[]{:S(2)}, u32[]{:S(2)}) collective-permute-start(bf16[32,128]{1,0:T(8,128)(2,1)S(1)} %get-tuple-element.27), channel_id=1, source_target_pairs={{0,30},{2,28},{4,26},{6,24},{8,22},{10,20},{12,18},{14,16},{16,14}... | collective-permute-start | bytes 24584 | tf_op jit(solution)/shard_map/ppermute | solution.py:266
  23.7 6.5 %collective-permute-start.5 = (bf16[32,128]{1,0:T(8,128)(2,1)S(1)}, bf16[32,128]{1,0:T(8,128)(2,1)S(1)}, u32[]{:S(2)}, u32[]{:S(2)}) collective-permute-start(bf16[32,128]{1,0:T(8,128)(2,1)S(1)} %get-tuple-element.26), channel_id=1, source_target_pairs={{0,12},{2,14},{4,8},{6,10},{8,4},{10,6},{12,0},{14,2},{16,28},{18,... | collective-permute-start | bytes 24584 | tf_op jit(solution)/shard_map/ppermute | solution.py:266
  42.6 6.6 %collective-permute-start.17 = (f32[40,128]{1,0:T(8,128)S(1)}, f32[40,128]{1,0:T(8,128)S(1)}, u32[]{:S(2)}, u32[]{:S(2)}) collective-permute-start(f32[40,128]{1,0:T(8,128)S(1)} %get-tuple-element.29), channel_id=1, source_target_pairs={{0,2},{2,0},{4,6},{6,4},{8,10},{10,8},{12,14},{14,12},{16,18},{18,... | collective-permute-start | bytes 61448 | tf_op jit(solution)/shard_map/ppermute | solution.py:266
  44.2 6.3 %collective-permute-start.18 = (f32[40,128]{1,0:T(8,128)S(1)}, f32[40,128]{1,0:T(8,128)S(1)}, u32[]{:S(2)}, u32[]{:S(2)}) collective-permute-start(f32[40,128]{1,0:T(8,128)S(1)} %get-tuple-element.30), channel_id=1, source_target_pairs={{0,4},{2,6},{4,0},{6,2},{8,12},{10,14},{12,8},{14,10},{16,20},{18,... | collective-permute-start | bytes 61448 | tf_op jit(solution)/shard_map/ppermute | solution.py:266
  44.8 7.2 %collective-permute-start.19 = (f32[40,128]{1,0:T(8,128)S(1)}, f32[40,128]{1,0:T(8,128)S(1)}, u32[]{:S(2)}, u32[]{:S(2)}) collective-permute-start(f32[40,128]{1,0:T(8,128)S(1)} %get-tuple-element.31), channel_id=1, source_target_pairs={{0,6},{2,4},{4,2},{6,0},{8,14},{10,12},{12,10},{14,8},{16,22},{18,... | collective-permute-start | bytes 61448 | tf_op jit(solution)/shard_map/ppermute | solution.py:266
  46.1 6.9 %collective-permute-start.20 = (f32[40,128]{1,0:T(8,128)S(1)}, f32[40,128]{1,0:T(8,128)S(1)}, u32[]{:S(2)}, u32[]{:S(2)}) collective-permute-start(f32[40,128]{1,0:T(8,128)S(1)} %get-tuple-element.32), channel_id=1, source_target_pairs={{0,8},{2,10},{4,12},{6,14},{8,0},{10,2},{12,4},{14,6},{16,24},{18,... | collective-permute-start | bytes 61448 | tf_op jit(solution)/shard_map/ppermute | solution.py:266
  46.6 9.4 %collective-permute-start.21 = (f32[40,128]{1,0:T(8,128)S(1)}, f32[40,128]{1,0:T(8,128)S(1)}, u32[]{:S(2)}, u32[]{:S(2)}) collective-permute-start(f32[40,128]{1,0:T(8,128)S(1)} %get-tuple-element.33), channel_id=1, source_target_pairs={{0,10},{2,8},{4,14},{6,12},{8,2},{10,0},{12,6},{14,4},{16,26},{18,... | collective-permute-start | bytes 61448 | tf_op jit(solution)/shard_map/ppermute | solution.py:266
  49.2 7.7 %collective-permute-start.22 = (f32[40,128]{1,0:T(8,128)S(1)}, f32[40,128]{1,0:T(8,128)S(1)}, u32[]{:S(2)}, u32[]{:S(2)}) collective-permute-start(f32[40,128]{1,0:T(8,128)S(1)} %get-tuple-element.34), channel_id=1, source_target_pairs={{0,12},{2,14},{4,8},{6,10},{8,4},{10,6},{12,0},{14,2},{16,28},{18,... | collective-permute-start | bytes 61448 | tf_op jit(solution)/shard_map/ppermute | solution.py:266
  50.5 9.2 %collective-permute-start.23 = (f32[40,128]{1,0:T(8,128)S(1)}, f32[40,128]{1,0:T(8,128)S(1)}, u32[]{:S(2)}, u32[]{:S(2)}) collective-permute-start(f32[40,128]{1,0:T(8,128)S(1)} %get-tuple-element.35), channel_id=1, source_target_pairs={{0,14},{2,12},{4,10},{6,8},{8,6},{10,4},{12,2},{14,0},{16,30},{18,... | collective-permute-start | bytes 61448 | tf_op jit(solution)/shard_map/ppermute | solution.py:266
  52.0 9.2 %collective-permute-start.24 = (f32[40,128]{1,0:T(8,128)S(1)}, f32[40,128]{1,0:T(8,128)S(1)}, u32[]{:S(2)}, u32[]{:S(2)}) collective-permute-start(f32[40,128]{1,0:T(8,128)S(1)} %get-tuple-element.36), channel_id=1, source_target_pairs={{0,16},{2,18},{4,20},{6,22},{8,24},{10,26},{12,28},{14,30},{16,0},... | collective-permute-start | bytes 61448 | tf_op jit(solution)/shard_map/ppermute | solution.py:266
  53.1 11.5 %collective-permute-start.25 = (f32[40,128]{1,0:T(8,128)S(1)}, f32[40,128]{1,0:T(8,128)S(1)}, u32[]{:S(2)}, u32[]{:S(2)}) collective-permute-start(f32[40,128]{1,0:T(8,128)S(1)} %get-tuple-element.37), channel_id=1, source_target_pairs={{0,18},{2,16},{4,22},{6,20},{8,26},{10,24},{12,30},{14,28},{16,2},... | collective-permute-start | bytes 61448 | tf_op jit(solution)/shard_map/ppermute | solution.py:266
  56.0 10.7 %collective-permute-start.26 = (f32[40,128]{1,0:T(8,128)S(1)}, f32[40,128]{1,0:T(8,128)S(1)}, u32[]{:S(2)}, u32[]{:S(2)}) collective-permute-start(f32[40,128]{1,0:T(8,128)S(1)} %get-tuple-element.38), channel_id=1, source_target_pairs={{0,20},{2,22},{4,16},{6,18},{8,28},{10,30},{12,24},{14,26},{16,4},... | collective-permute-start | bytes 61448 | tf_op jit(solution)/shard_map/ppermute | solution.py:266
  56.9 19.5 %collective-permute-start.27 = (f32[40,128]{1,0:T(8,128)S(1)}, f32[40,128]{1,0:T(8,128)S(1)}, u32[]{:S(2)}, u32[]{:S(2)}) collective-permute-start(f32[40,128]{1,0:T(8,128)S(1)} %get-tuple-element.39), channel_id=1, source_target_pairs={{0,22},{2,20},{4,18},{6,16},{8,30},{10,28},{12,26},{14,24},{16,6},... | collective-permute-start | bytes 61448 | tf_op jit(solution)/shard_map/ppermute | solution.py:266
  59.7 16.7 %collective-permute-start.28 = (f32[40,128]{1,0:T(8,128)S(1)}, f32[40,128]{1,0:T(8,128)S(1)}, u32[]{:S(2)}, u32[]{:S(2)}) collective-permute-start(f32[40,128]{1,0:T(8,128)S(1)} %get-tuple-element.40), channel_id=1, source_target_pairs={{0,24},{2,26},{4,28},{6,30},{8,16},{10,18},{12,20},{14,22},{16,8},... | collective-permute-start | bytes 61448 | tf_op jit(solution)/shard_map/ppermute | solution.py:266
  61.2 15.2 %collective-permute-start.29 = (f32[40,128]{1,0:T(8,128)S(1)}, f32[40,128]{1,0:T(8,128)S(1)}, u32[]{:S(2)}, u32[]{:S(2)}) collective-permute-start(f32[40,128]{1,0:T(8,128)S(1)} %get-tuple-element.41), channel_id=1, source_target_pairs={{0,26},{2,24},{4,30},{6,28},{8,18},{10,16},{12,22},{14,20},{16,10}... | collective-permute-start | bytes 61448 | tf_op jit(solution)/shard_map/ppermute | solution.py:266
  64.5 11.9 %collective-permute-start.30 = (f32[40,128]{1,0:T(8,128)S(1)}, f32[40,128]{1,0:T(8,128)S(1)}, u32[]{:S(2)}, u32[]{:S(2)}) collective-permute-start(f32[40,128]{1,0:T(8,128)S(1)} %get-tuple-element.42), channel_id=1, source_target_pairs={{0,28},{2,30},{4,24},{6,26},{8,20},{10,22},{12,16},{14,18},{16,12}... | collective-permute-start | bytes 61448 | tf_op jit(solution)/shard_map/ppermute | solution.py:266
  66.6 9.8 %collective-permute-start.31 = (f32[40,128]{1,0:T(8,128)S(1)}, f32[40,128]{1,0:T(8,128)S(1)}, u32[]{:S(2)}, u32[]{:S(2)}) collective-permute-start(f32[40,128]{1,0:T(8,128)S(1)} %get-tuple-element.43), channel_id=1, source_target_pairs={{0,30},{2,28},{4,26},{6,24},{8,22},{10,20},{12,18},{14,16},{16,14}... | collective-permute-start | bytes 61448 | tf_op jit(solution)/shard_map/ppermute | solution.py:266
  (13 other events, 46.9 us)
